TPU v7x, 32 devices: a whole 2x2x4 slice. The times are simulated.
32 devices in a mesh: groups: 2 (over y), ctx: 4 (over z), head: 4 (over x, core).
Axes of the slice: x: 2, y: 2, z: 4, core: 2. Of those that a mesh axis runs over, the one named last changes fastest.
Arguments:
- query_rows: bfloat16 [3072, 3072], P(('groups', 'ctx', 'head')), parts along dimension 0, may hold values from -150 to 150
- key_rows: bfloat16 [3072, 3072], P(('groups', 'ctx', 'head')), parts along dimension 0, may hold values from -6 to 6
- value_rows: bfloat16 [3072, 3072], P(('groups', 'ctx', 'head')), parts along dimension 0, may hold values from -6 to 6
- tile_mask: int32 [8, 27], P(('groups', 'ctx')), parts along dimension 0, may hold values from 0 to 1, as said below
Outputs:
- attended: bfloat16 [3072, 3072], P(('groups', 'ctx', 'head')), parts along dimension 0
There are 2 independent parts, one for each index of `groups`. A program takes and returns all parts, laid end to end along the dimension named above; each array names one. Nothing has to cross between parts.
Inputs may be any that keep to these rules, and one draw needn't show every extreme that they name: `tile_mask`: entry o of row i is 1 only where the key tile of offset o lies inside the grid; entry 13 is always 1; a row has at most 4 ones, and some row has exactly 4.
All inputs are finite; a program needn't handle non-finite values.
Results may differ from a plain program's by a relative error of at most 0.0023.
Values may be sent and summed in bfloat16 or wider, within the bound.
A program may use at most 64 MiB of HBM per device.

v0:
```python
import math

import jax
import jax.numpy as jnp
from jax import lax
from jax.sharding import PartitionSpec as P

HDIM = 128


def passed_along(block, axis, distance):
    devices = range(lax.axis_size(axis))
    route = [((i - distance) % len(devices), i) for i in devices]
    return lax.ppermute(block, axis, route)


def on_device(query_rows, key_rows, value_rows, tile_mask):
    cycle_size = lax.axis_size("ctx")
    grid_rows = max(2, cycle_size // 8)
    grid_cols = cycle_size // grid_rows
    query_local, key_local, value_local = (
        lax.all_to_all(query_rows, "head", split_axis=1, concat_axis=0, tiled=True),
        lax.all_to_all(key_rows, "head", split_axis=1, concat_axis=0, tiled=True),
        lax.all_to_all(value_rows, "head", split_axis=1, concat_axis=0, tiled=True),
    )
    feature_width = query_local.shape[1]
    head_count = feature_width // HDIM
    frames = tile_mask.shape[0]
    tile_len = query_local.shape[0] // frames
    key_value = jnp.stack([key_local, value_local]).reshape(2, frames, tile_len, feature_width)
    row_parts = [passed_along(key_value, "ctx", shift_by) for shift_by in (1, -1)]
    row_strip = jnp.stack([row_parts[0], key_value, row_parts[1]])
    column_parts = [
        passed_along(row_strip, "ctx", shift_by) for shift_by in (grid_cols, -grid_cols)
    ]
    window = jnp.stack([column_parts[0], row_strip, column_parts[1]])
    key_tiles = window[:, :, 0].reshape(9 * frames, tile_len, feature_width)
    value_tiles = window[:, :, 1].reshape(9 * frames, tile_len, feature_width)
    kept_mask = tile_mask == 1
    first_offset = 9
    slot_count = 9
    slot_order = jnp.arange(first_offset, first_offset + slot_count, dtype=jnp.int32)[None, :]
    slot_kept = kept_mask[:, first_offset : first_offset + slot_count]
    frame_ids = jnp.arange(frames, dtype=jnp.int32)[:, None]
    source_frame = jnp.clip(frame_ids + slot_order // 9 - 1, 0, frames - 1)
    source = slot_order % 9 * frames + source_frame
    kept_cols = jnp.repeat(slot_kept, tile_len, axis=1)[:, None, :]
    score_scale = 1.0 / math.sqrt(HDIM)

    def one_head(head_index):
        column_start = head_index * HDIM
        key_head = lax.dynamic_slice_in_dim(key_tiles, column_start, HDIM, 2)
        value_head = lax.dynamic_slice_in_dim(value_tiles, column_start, HDIM, 2)
        query_head = lax.dynamic_slice_in_dim(query_local, column_start, HDIM, 1).reshape(
            frames, tile_len, HDIM
        )
        picked_keys = jnp.take(key_head, source, axis=0).reshape(
            frames, slot_count * tile_len, HDIM
        )
        picked_values = jnp.take(value_head, source, axis=0).reshape(
            frames, slot_count * tile_len, HDIM
        )
        scores = (
            jnp.einsum("fqd,fkd->fqk", query_head, picked_keys, preferred_element_type=jnp.float32)
            * score_scale
        )
        row_peak = jnp.max(jnp.where(kept_cols, scores, -jnp.inf), axis=2, keepdims=True)
        weight = jnp.exp(jnp.where(kept_cols, scores - row_peak, -jnp.inf))
        row_total = jnp.sum(weight, axis=2, keepdims=True)
        rounded = weight.astype(jnp.bfloat16)
        mixed = jnp.einsum(
            "fqk,fkd->fqd", rounded, picked_values, preferred_element_type=jnp.float32
        )
        return (mixed / row_total).astype(jnp.bfloat16)

    result = lax.map(one_head, jnp.arange(head_count, dtype=jnp.int32))
    result = jnp.transpose(result, (1, 2, 0, 3)).reshape(frames * tile_len, feature_width)
    return lax.all_to_all(result, "head", split_axis=0, concat_axis=1, tiled=True)


def solution(mesh):
    placed = (
        P(("groups", "ctx", "head"), None),
        P(("groups", "ctx", "head"), None),
        P(("groups", "ctx", "head"), None),
        P(("groups", "ctx"), None),
    )
    return jax.shard_map(
        on_device,
        mesh=mesh,
        in_specs=placed,
        out_specs=P(("groups", "ctx", "head"), None),
        check_vma=False,
    )
```

profile of v0, /device:TPU:0, one launch (start us, length us, event | category | flops | bytes accessed | tf_op | source)
XLA Modules:
  0.0 327.5 jit_solution(2252575000279086143)
XLA Ops:
  0.0 1.9 copy.44
  1.9 4.2 %all-to-all-start.1 = ((bf16[96,4,768]{2,0,1:T(8,128)(2,1)}), bf16[96,4,768]{2,0,1:T(8,128)(2,1)S(1)}, u32[]{:S(2)}, u32[]{:S(2)}) async-start(bf16[96,4,768]{2,0,1:T(8,128)(2,1)} %bitcast.57), calls=%async_computation.1 | async-start | bytes 1179648 | tf_op jit(solution)/shard_map/all_to_all | solution.py:23
  6.1 1.1 copy.43
  7.2 8.4 %all-to-all-done.1 = bf16[96,4,768]{2,0,1:T(8,128)(2,1)S(1)} async-done(((bf16[96,4,768]{2,0,1:T(8,128)(2,1)}), bf16[96,4,768]{2,0,1:T(8,128)(2,1)S(1)}, u32[]{:S(2)}, u32[]{:S(2)}) %all-to-all-start.1) | async-done | bytes 589856 | tf_op jit(solution)/shard_map/all_to_all | solution.py:23
  15.7 11.9 %all_to_all.70 = bf16[96,4,768]{2,0,1:T(8,128)(2,1)S(1)} all-to-all(bf16[96,4,768]{2,0,1:T(8,128)(2,1)S(1)} %bitcast.84), channel_id=1, replica_groups=mesh['groups'=2,'ctx'=4,'head'=4] {'head'}, dimensions={1} | all-to-all | bytes 1179648 | tf_op jit(solution)/shard_map/all_to_all | solution.py:24
  27.8 2.3 collective-permute-start
  30.1 2.1 collective-permute-start.1
  32.2 26.8 %collective-permute-done = bf16[2,1,384,768]{3,2,0,1:T(8,128)(2,1)S(1)} collective-permute-done((bf16[2,1,384,768]{3,2,0,1:T(8,128)(2,1)S(1)}, bf16[2,1,384,768]{3,2,0,1:T(8,128)(2,1)S(1)}, u32[]{:S(2)}, u32[]{:S(2)}) %collective-permute-start) | collective-permute-done | bytes 1179680 | tf_op jit(solution)/shard_map/ppermute | solution.py:14
  58.9 23.8 %collective-permute-done.1 = bf16[2,1,384,768]{3,2,0,1:T(8,128)(2,1)S(1)} collective-permute-done((bf16[2,1,384,768]{3,2,0,1:T(8,128)(2,1)S(1)}, bf16[2,1,384,768]{3,2,0,1:T(8,128)(2,1)S(1)}, u32[]{:S(2)}, u32[]{:S(2)}) %collective-permute-start.1) | collective-permute-done | bytes 1179680 | tf_op jit(solution)/shard_map/ppermute | solution.py:14
  82.7 2.0 fusion.32
  84.7 1.3 collective-permute-start.2
  86.0 0.9 copy.45
  86.9 4.2 %all-to-all-start = ((bf16[96,4,768]{2,0,1:T(8,128)(2,1)}), bf16[96,4,768]{2,0,1:T(8,128)(2,1)}, u32[]{:S(2)}, u32[]{:S(2)}) async-start(bf16[96,4,768]{2,0,1:T(8,128)(2,1)} %bitcast.83), calls=%async_computation | async-start | bytes 1179648 | tf_op jit(solution)/shard_map/all_to_all | solution.py:22
  91.2 148.4 %collective-permute-done.2 = bf16[3,2,1,384,768]{4,3,1,0,2:T(8,128)(2,1)} collective-permute-done((bf16[3,2,1,384,768]{4,3,1,0,2:T(8,128)(2,1)}, bf16[3,2,1,384,768]{4,3,1,0,2:T(8,128)(2,1)}, u32[]{:S(2)}, u32[]{:S(2)}) %collective-permute-start.2) | collective-permute-done | bytes 3538976 | tf_op jit(solution)/shard_map/ppermute | solution.py:14
  239.6 8.4 %pad_maximum_fusion = bf16[3,3,2,1,384,768]{5,4,2,1,3,0:T(8,128)(2,1)} fusion(bf16[1,3,2,1,384,768]{5,4,2,1,3,0:T(8,128)(2,1)} %bitcast.11, bf16[1,3,2,1,384,768]{5,4,2,1,3,0:T(8,128)(2,1)S(1)} %get-tuple-element.112), kind=kLoop, calls=%fused_computation.36 | loop fusion | flops 10616832 | bytes 17694720 | tf_op jit(solution)/shard_map/stack | solution.py:36
  248.0 8.9 %fusion.36 = (bf16[3,3,1,1,384,768]{5,4,2,1,3,0:T(8,128)(2,1)}, bf16[3,3,1,1,384,768]{5,4,2,1,3,0:T(8,128)(2,1)}) fusion(bf16[3,3,2,1,384,768]{5,4,2,1,3,0:T(8,128)(2,1)} %pad_maximum_fusion), kind=kLoop, calls=%fused_computation.48 | loop fusion | bytes 21233664 | tf_op jit(solution)/shard_map/slice | solution.py:38
  256.9 55.6 %while.12 = (s32[]{:T(128)}, bf16[6,1,384,128]{3,2,1,0:T(8,128)(2,1)}, s32[6]{0:T(128)S(1)}, bf16[384,768]{1,0:T(8,128)(2,1)}, bf16[9,384,768]{2,1,0:T(8,128)(2,...) while((s32[]{:T(128)}, ...), condition=%wide.region_3.5_spmd.clone.clone, body=%wide.region_0.4_spmd.clone.clone.sunk | while | flops 692404736 | bytes 28541528 | solution.py:76
  256.9 0.6 dynamic_slice.32
  258.2 1.6 constant_dynamic-slice_fusion.3
  259.8 0.7 gather_fusion
  260.5 0.7 gather_fusion.1
  261.6 1.9 select_reduce_fusion.2
  263.4 1.1 fusion.49
  264.5 1.6 fusion.50
  266.2 0.6 dynamic_slice.32
  267.4 1.6 constant_dynamic-slice_fusion.3
  269.0 0.7 gather_fusion
  269.8 0.7 gather_fusion.1
  270.5 0.2 bitcast_select_fusion.3
  270.8 1.9 select_reduce_fusion.2
  272.7 1.1 fusion.49
  273.8 1.6 fusion.50
  275.4 0.6 dynamic_slice.32
  276.7 1.6 constant_dynamic-slice_fusion.3
  278.3 0.7 gather_fusion
  279.0 0.7 gather_fusion.1
  280.1 1.9 select_reduce_fusion.2
  282.0 1.1 fusion.49
  283.1 1.6 fusion.50
  284.7 0.6 dynamic_slice.32
  286.0 1.6 constant_dynamic-slice_fusion.3
  287.6 0.7 gather_fusion
  288.3 0.7 gather_fusion.1
  289.4 1.9 select_reduce_fusion.2
  291.2 1.1 fusion.49
  292.3 1.6 fusion.50
  294.0 0.6 dynamic_slice.32
  295.2 1.6 constant_dynamic-slice_fusion.3
  296.8 0.7 gather_fusion
  297.6 0.7 gather_fusion.1
  298.6 1.9 select_reduce_fusion.2
  300.5 1.1 fusion.49
  301.6 1.6 fusion.50
  303.2 0.6 dynamic_slice.32
  304.5 1.6 constant_dynamic-slice_fusion.3
  306.1 0.7 gather_fusion
  306.8 0.7 gather_fusion.1
  307.9 1.9 select_reduce_fusion.2
  309.8 1.1 fusion.49
  310.9 1.6 fusion.50
  312.5 1.5 copy.34
  314.0 0.7 all_to_all.62
  314.7 11.9 %all_to_all.71 = bf16[4,96,768]{2,1,0:T(8,128)(2,1)S(1)} all-to-all(bf16[4,96,768]{2,1,0:T(8,128)(2,1)S(1)} %all_to_all.62), channel_id=1, replica_groups=mesh['groups'=2,'ctx'=4,'head'=4] {'head'}, dimensions={0} | all-to-all | bytes 1179648 | tf_op jit(solution)/shard_map/all_to_all | solution.py:78
  326.6 0.9 copy.39
  (45 shorter events, 2.1 us)
Async XLA Ops:
  1.9 13.8 %all-to-all-start.1 = ((bf16[96,4,768]{2,0,1:T(8,128)(2,1)}), bf16[96,4,768]{2,0,1:T(8,128)(2,1)S(1)}, u32[]{:S(2)}, u32[]{:S(2)}) async-start(bf16[96,4,768]{2,0,1:T(8,128)(2,1)} %bitcast.57), calls=%async_computation.1 | async-start | bytes 1179648 | tf_op jit(solution)/shard_map/all_to_all | solution.py:23
  27.8 31.2 %collective-permute-start = (bf16[2,1,384,768]{3,2,0,1:T(8,128)(2,1)S(1)}, bf16[2,1,384,768]{3,2,0,1:T(8,128)(2,1)S(1)}, u32[]{:S(2)}, u32[]{:S(2)}) collective-permute-start(bf16[2,1,384,768]{3,2,0,1:T(8,128)(2,1)S(1)} %get-tuple-element.115), channel_id=1, source_target_pairs={{12,0},{0,4},{4,8},{8,12},{13,1},{1,5},{5,9},{9,13},{14,2},{2,6},{... | collective-permute-start | bytes 3538952 | tf_op jit(solution)/shard_map/ppermute | solution.py:14
  30.1 52.6 %collective-permute-start.1 = (bf16[2,1,384,768]{3,2,0,1:T(8,128)(2,1)S(1)}, bf16[2,1,384,768]{3,2,0,1:T(8,128)(2,1)S(1)}, u32[]{:S(2)}, u32[]{:S(2)}) collective-permute-start(bf16[2,1,384,768]{3,2,0,1:T(8,128)(2,1)S(1)} %get-tuple-element.115), channel_id=1, source_target_pairs={{4,0},{8,4},{12,8},{0,12},{5,1},{9,5},{13,9},{1,13},{6,2},{10,6},{... | collective-permute-start | bytes 3538952 | tf_op jit(solution)/shard_map/ppermute | solution.py:14
  82.7 3.3 %copy-start = (bf16[96,3072]{1,0:T(8,128)(2,1)S(1)}, bf16[96,3072]{1,0:T(8,128)(2,1)}, u32[]{:S(2)}) copy-start(bf16[96,3072]{1,0:T(8,128)(2,1)} %param.8) | copy-start | bytes 1769476
  82.7 8.4 %copy-start.1 = (s32[1,27]{1,0:T(1,128)S(1)}, s32[1,27]{1,0:T(1,128)}, u32[]{:S(2)}) copy-start(s32[1,27]{1,0:T(1,128)} %param.11) | copy-start | bytes 328
  84.7 154.9 %collective-permute-start.2 = (bf16[3,2,1,384,768]{4,3,1,0,2:T(8,128)(2,1)}, bf16[3,2,1,384,768]{4,3,1,0,2:T(8,128)(2,1)}, u32[]{:S(2)}, u32[]{:S(2)}) collective-permute-start(bf16[3,2,1,384,768]{4,3,1,0,2:T(8,128)(2,1)} %get-tuple-element.113), channel_id=1, source_target_pairs={{8,0},{12,4},{0,8},{4,12},{9,1},{13,5},{1,9},{5,13},{10,2},{14,6},... | collective-permute-start | bytes 10616840 | tf_op jit(solution)/shard_map/ppermute | solution.py:14
  86.9 170.0 %all-to-all-start = ((bf16[96,4,768]{2,0,1:T(8,128)(2,1)}), bf16[96,4,768]{2,0,1:T(8,128)(2,1)}, u32[]{:S(2)}, u32[]{:S(2)}) async-start(bf16[96,4,768]{2,0,1:T(8,128)(2,1)} %bitcast.83), calls=%async_computation | async-start | bytes 1179648 | tf_op jit(solution)/shard_map/all_to_all | solution.py:22
where the time goes:
time: 328 us; the launch traced here: 327 us
  waiting for transfers between devices  207 us (63%)
  local copies, waits for them, and re-layouts  38.3 us (12%)
  blocking collectives  23.9 us (7%)
  matrix products  21 us (6%)
  other arithmetic  18.6 us (6%)
  starting transfers between devices  14.1 us (4%)
  loops' own time  4.07 us (1%)
    ppermute x3, waiting for transfers between devices, passed_along(): return lax.ppermute(block, axis, route)  199 us
    all_to_all x1, blocking collectives, on_device(): lax.all_to_all(result, 'head', split_axis=0, concat_axis=1, tiled=True)  11.9 us
    all_to_all x1, blocking collectives, on_device(): lax.all_to_all(value_rows, 'head', split_axis=1, concat_axis=0, tiled=True)  11.9 us
    dot_general x6, matrix products, one_head(): jnp.einsum('fqd,fkd->fqk', query_head, picked_keys, preferred_element_typ...  11.2 us
    another operation x2, other arithmetic, on_device(): window = jnp.stack([column_parts[0], row_strip, column_parts[1]])  10.4 us
    dot_general x6, matrix products, one_head(): jnp.einsum('fqk,fkd->fqd', rounded, picked_values, preferred_element_type...  9.83 us
    dynamic_slice x6, local copies, waits for them, and re-layouts, one_head(): value_head = lax.dynamic_slice_in_dim(value_tiles, column_start, HDIM, 2)  9.42 us
    slice x1, local copies, waits for them, and re-layouts, on_device(): value_tiles = window[:, :, 1].reshape(9 * frames, tile_len, feature_width)  8.9 us
  transfers between devices with their start and end apart: 5, of which 4 were waited for; matrix products, arithmetic and copies ran while one was open for 6% of the time, Pallas kernels for 0%

commit v1 on v0

--- a/solution.py
+++ b/solution.py
@@ -1,8 +1,11 @@
+import functools
 import math
 
 import jax
 import jax.numpy as jnp
 from jax import lax
+from jax.experimental import pallas as pl
+from jax.experimental.pallas import tpu as pltpu
 from jax.sharding import PartitionSpec as P
 
 HDIM = 128
@@ -39,13 +42,19 @@
     kept_mask = tile_mask == 1
     first_offset = 9
     slot_count = 9
-    slot_order = jnp.arange(first_offset, first_offset + slot_count, dtype=jnp.int32)[None, :]
+    slots = range(first_offset, first_offset + slot_count)
     slot_kept = kept_mask[:, first_offset : first_offset + slot_count]
-    frame_ids = jnp.arange(frames, dtype=jnp.int32)[:, None]
-    source_frame = jnp.clip(frame_ids + slot_order // 9 - 1, 0, frames - 1)
-    source = slot_order % 9 * frames + source_frame
+    static_source = [
+        [slot % 9 * frames + min(max(frame + slot // 9 - 1, 0), frames - 1) for slot in slots]
+        for frame in range(frames)
+    ]
     kept_cols = jnp.repeat(slot_kept, tile_len, axis=1)[:, None, :]
     score_scale = 1.0 / math.sqrt(HDIM)
+
+    def picked(tiles):
+        return jnp.stack(
+            [jnp.concatenate([tiles[tile] for tile in row]) for row in static_source]
+        )
 
     def one_head(head_index):
         column_start = head_index * HDIM
@@ -54,12 +63,8 @@
         query_head = lax.dynamic_slice_in_dim(query_local, column_start, HDIM, 1).reshape(
             frames, tile_len, HDIM
         )
-        picked_keys = jnp.take(key_head, source, axis=0).reshape(
-            frames, slot_count * tile_len, HDIM
-        )
-        picked_values = jnp.take(value_head, source, axis=0).reshape(
-            frames, slot_count * tile_len, HDIM
-        )
+        picked_keys = picked(key_head)
+        picked_values = picked(value_head)
         scores = (
             jnp.einsum("fqd,fkd->fqk", query_head, picked_keys, preferred_element_type=jnp.float32)
             * score_scale
@@ -76,6 +81,271 @@
     result = lax.map(one_head, jnp.arange(head_count, dtype=jnp.int32))
     result = jnp.transpose(result, (1, 2, 0, 3)).reshape(frames * tile_len, feature_width)
     return lax.all_to_all(result, "head", split_axis=0, concat_axis=1, tiled=True)
+
+
+MESH = pl.DeviceIdType.MESH
+MASKED = -1e30
+
+
+def window_kernel(
+    places, heads, q_ref, k_ref, v_ref, m_ref, out_ref, qbuf, kvbuf, obuf, mbuf, bias,
+    in_send, in_recv, own_sem, pair_send, pair_recv, o_send, o_recv, o_own, m_send, m_recv,
+):
+    tiles, chips = places
+    blocks = tiles * chips
+    rows = q_ref.shape[0]
+    tile_rows = chips * rows
+    z = lax.axis_index("ctx")
+    lane = lax.axis_index("head")
+    x = lax.div(lane, 2)
+    core = lax.rem(lane, 2)
+    here = z * chips + x
+
+    def peer(dz, dx):
+        pz = lax.rem(z + dz, tiles)
+        px = lax.rem(x + dx, chips)
+        return pz * chips + px, {"ctx": pz, "head": px * 2 + core}
+
+    sibling = {"ctx": z, "head": x * 2 + 1 - core}
+    distances = [2, 1, 3, 0]
+    offsets = [(dz, dx) for dz in distances for dx in range(chips) if (dz, dx) != (0, 0)]
+
+    def columns(place, h):
+        return pl.ds(pl.multiple_of((place * heads + h) * HDIM, HDIM), HDIM)
+
+    def slot(kind, h, place):
+        if kind == 2:
+            return qbuf.at[h, pl.ds(pl.multiple_of(place * rows, 16), rows)]
+        return kvbuf.at[h, core, kind, pl.ds(pl.multiple_of(place * rows, 16), rows)]
+
+    sources = (k_ref, v_ref, q_ref)
+
+    def own_copy(kind, h):
+        return pltpu.make_async_copy(
+            sources[kind].at[:, columns(here, h)], slot(kind, h, here), own_sem.at[h, kind]
+        )
+
+    def in_copy(kind, h, offset):
+        place, device = peer(*offset)
+        return pltpu.make_async_remote_copy(
+            src_ref=sources[kind].at[:, columns(place, h)],
+            dst_ref=slot(kind, h, here),
+            send_sem=in_send.at[h, kind, place],
+            recv_sem=in_recv.at[h, kind, here],
+            device_id=device,
+            device_id_type=MESH,
+        )
+
+    def in_arrival(kind, h, offset):
+        place, device = peer(*offset)
+        return pltpu.make_async_remote_copy(
+            src_ref=sources[kind].at[:, columns(place, h)],
+            dst_ref=slot(kind, h, place),
+            send_sem=in_send.at[h, kind, place],
+            recv_sem=in_recv.at[h, kind, place],
+            device_id=device,
+            device_id_type=MESH,
+        )
+
+    def mask_copy(dz, sender):
+        pz = lax.rem(z + dz, tiles)
+        return pltpu.make_async_remote_copy(
+            src_ref=mbuf.at[z],
+            dst_ref=mbuf.at[z if sender else pz],
+            send_sem=m_send.at[pz],
+            recv_sem=m_recv.at[z if sender else pz],
+            device_id={"ctx": pz, "head": lane},
+            device_id_type=MESH,
+        )
+
+    def pair_copy(h, side):
+        return pltpu.make_async_remote_copy(
+            src_ref=kvbuf.at[h, core],
+            dst_ref=kvbuf.at[h, side],
+            send_sem=pair_send.at[h],
+            recv_sem=pair_recv.at[h],
+            device_id=sibling,
+            device_id_type=MESH,
+        )
+
+    def out_copy(h, pz, px):
+        place = pz * chips + px
+        return pltpu.make_async_remote_copy(
+            src_ref=obuf.at[h, pl.ds(pl.multiple_of(place * rows, 16), rows)],
+            dst_ref=out_ref.at[:, columns(here, h)],
+            send_sem=o_send.at[h, place],
+            recv_sem=o_recv.at[h, here],
+            device_id={"ctx": pz, "head": px * 2 + core},
+            device_id_type=MESH,
+        )
+
+    def out_arrival(h, offset):
+        place, device = peer(*offset)
+        return pltpu.make_async_remote_copy(
+            src_ref=obuf.at[h, pl.ds(pl.multiple_of(place * rows, 16), rows)],
+            dst_ref=out_ref.at[:, columns(place, h)],
+            send_sem=o_send.at[h, place],
+            recv_sem=o_recv.at[h, place],
+            device_id=device,
+            device_id_type=MESH,
+        )
+
+    def out_own(h):
+        return pltpu.make_async_copy(
+            obuf.at[h, pl.ds(pl.multiple_of(here * rows, 16), rows)],
+            out_ref.at[:, columns(here, h)],
+            o_own.at[h],
+        )
+
+    barrier = pltpu.get_barrier_semaphore()
+    for offset in offsets:
+        pl.semaphore_signal(barrier, inc=1, device_id=peer(*offset)[1], device_id_type=MESH)
+    pl.semaphore_signal(barrier, inc=1, device_id=sibling, device_id_type=MESH)
+
+    mbuf[z] = jnp.zeros(mbuf.shape[1:], mbuf.dtype)
+    mbuf[z, 0:1, 0 : m_ref.shape[1]] = m_ref[...]
+    pl.semaphore_wait(barrier, len(offsets) + 1)
+
+    def start_head(h, carry):
+        for kind in range(3):
+            for offset in offsets:
+                in_copy(kind, h, offset).start()
+            own_copy(kind, h).start()
+        return carry
+
+    start_head(0, 0)
+    for dz in distances[:-1]:
+        mask_copy(dz, True).start()
+    lax.fori_loop(1, heads, start_head, 0)
+
+    for dz in distances[:-1]:
+        mask_copy(dz, False).wait_recv()
+    grid_cols = 2
+    spot = lax.broadcasted_iota(jnp.int32, (1, blocks * rows), 1)
+    for query in range(tiles):
+        query_spot = (query - grid_cols // 2) % tiles
+        kept = mbuf[query][0:1, :]
+        row = jnp.zeros((1, blocks * rows), jnp.float32)
+        for key in range(tiles):
+            key_spot = (key - grid_cols // 2) % tiles
+            step_row = key_spot // grid_cols - query_spot // grid_cols
+            step_col = key_spot % grid_cols - query_spot % grid_cols
+            entry = 9 + 3 * (step_row + 1) + step_col + 1
+            inside = (spot >= key * tile_rows) & (spot < (key + 1) * tile_rows)
+            dropped = jnp.where(kept[:, entry : entry + 1] == 1, 0.0, MASKED)
+            row = jnp.where(inside, dropped, row)
+        bias[query] = row
+
+    factor = math.log2(math.e) / math.sqrt(HDIM)
+
+    def attend(h, pz):
+        start = pl.multiple_of(pz * tile_rows, 16)
+        query = qbuf[h, pl.ds(start, tile_rows), :]
+        extra = bias[pz]
+        scores = [
+            lax.dot_general(
+                query, kvbuf[h, side, 0], (((1,), (1,)), ((), ())),
+                preferred_element_type=jnp.float32,
+            )
+            + extra
+            for side in range(2)
+        ]
+        peak = jnp.maximum(*[jnp.max(s, axis=1, keepdims=True) for s in scores])
+        weights = [jnp.exp2((s - peak) * factor) for s in scores]
+        total = sum(jnp.sum(w, axis=1, keepdims=True) for w in weights)
+        mixed = sum(
+            jnp.dot(
+                weights[side].astype(jnp.bfloat16), kvbuf[h, side, 1],
+                preferred_element_type=jnp.float32,
+            )
+            for side in range(2)
+        )
+        obuf[h, pl.ds(start, tile_rows), :] = (mixed / total).astype(jnp.bfloat16)
+
+    def run_head(h, carry):
+        for kind in range(2):
+            for offset in offsets:
+                in_arrival(kind, h, offset).wait_recv()
+            own_copy(kind, h).wait()
+        pair_copy(h, core).start()
+        for offset in offsets:
+            in_arrival(2, h, offset).wait_recv()
+        own_copy(2, h).wait()
+        pair_copy(h, 1 - core).wait_recv()
+
+        def run_tile(i, carry):
+            pz = lax.rem(z + 2 + i, tiles)
+            attend(h, pz)
+            for px in range(chips):
+                mine = pz * chips + px == here
+
+                @pl.when(jnp.logical_not(mine))
+                def _():
+                    out_copy(h, pz, px).start()
+
+                @pl.when(mine)
+                def _():
+                    out_own(h).start()
+
+            return carry
+
+        return lax.fori_loop(0, tiles, run_tile, carry)
+
+    lax.fori_loop(0, heads, run_head, 0)
+
+    def finish_head(h, carry):
+        for kind in range(3):
+            for offset in offsets:
+                in_copy(kind, h, offset).wait_send()
+        pair_copy(h, core).wait_send()
+        for offset in offsets:
+            out_arrival(h, offset).wait_send()
+            out_arrival(h, offset).wait_recv()
+        out_own(h).wait()
+        return carry
+
+    for dz in distances[:-1]:
+        mask_copy(dz, True).wait_send()
+    lax.fori_loop(0, heads, finish_head, 0)
+
+
+def one_kernel(query_rows, key_rows, value_rows, tile_mask):
+    tiles = lax.axis_size("ctx")
+    chips = lax.axis_size("head") // 2
+    blocks = tiles * chips
+    rows, width = query_rows.shape
+    heads = width // HDIM // blocks
+    flops = 8 * heads * blocks * rows * blocks * rows * HDIM
+    return pl.pallas_call(
+        functools.partial(window_kernel, (tiles, chips), heads),
+        out_shape=jax.ShapeDtypeStruct((rows, width), jnp.bfloat16),
+        in_specs=[pl.BlockSpec(memory_space=pl.ANY)] * 3
+        + [pl.BlockSpec(memory_space=pltpu.VMEM)],
+        out_specs=pl.BlockSpec(memory_space=pltpu.VMEM),
+        scratch_shapes=[
+            pltpu.VMEM((heads, blocks * rows, HDIM), jnp.bfloat16),
+            pltpu.VMEM((heads, 2, 2, blocks * rows, HDIM), jnp.bfloat16),
+            pltpu.VMEM((heads, blocks * rows, HDIM), jnp.bfloat16),
+            pltpu.VMEM((tiles, 8, 128), jnp.int32),
+            pltpu.VMEM((tiles, 1, blocks * rows), jnp.float32),
+            pltpu.SemaphoreType.DMA((heads, 3, blocks)),
+            pltpu.SemaphoreType.DMA((heads, 3, blocks)),
+            pltpu.SemaphoreType.DMA((heads, 3)),
+            pltpu.SemaphoreType.DMA((heads,)),
+            pltpu.SemaphoreType.DMA((heads,)),
+            pltpu.SemaphoreType.DMA((heads, blocks)),
+            pltpu.SemaphoreType.DMA((heads, blocks)),
+            pltpu.SemaphoreType.DMA((heads,)),
+            pltpu.SemaphoreType.DMA((tiles,)),
+            pltpu.SemaphoreType.DMA((tiles,)),
+        ],
+        compiler_params=pltpu.CompilerParams(
+            collective_id=0, has_side_effects=True, vmem_limit_bytes=48 * 1024 * 1024
+        ),
+        cost_estimate=pl.CostEstimate(
+            flops=flops, bytes_accessed=8 * rows * width, transcendentals=0
+        ),
+    )(query_rows, key_rows, value_rows, tile_mask)
 
 
 def solution(mesh):
@@ -85,8 +355,10 @@
         P(("groups", "ctx", "head"), None),
         P(("groups", "ctx"), None),
     )
+    small = mesh.shape["ctx"] == 4 and mesh.shape["head"] % 2 == 0
+    body = one_kernel if small else on_device
     return jax.shard_map(
-        on_device,
+        body,
         mesh=mesh,
         in_specs=placed,
         out_specs=P(("groups", "ctx", "head"), None),

time: 328 us -> 64.6 us (0.20)
  waiting for transfers between devices: 207 us -> 0 us
  Pallas kernels: 0 us -> 59.7 us
  local copies, waits for them, and re-layouts: 38.3 us -> 4.66 us
  blocking collectives: 23.9 us -> 0 us
  matrix products: 21 us -> 0 us
  other arithmetic: 18.6 us -> 0 us
  starting transfers between devices: 14.1 us -> 0 us
  loops' own time: 4.07 us -> 0 us
    ppermute x3 -> x0, waiting for transfers between devices: 199 us -> none  [passed_along(): return lax.ppermute(block, axis, route)]
    pallas_call x0 -> x1, Pallas kernels: none -> 59.7 us  [one_kernel(): pl.pallas_call(functools.partial(window_kernel, (tiles, chips), heads), o...]
    all_to_all x2 -> x0, blocking collectives: 23.9 us -> none  [the longest x1 11.9 us: on_device(): lax.all_to_all(result, 'head', split_axis=0, concat_axis=1, tiled=True)]
    dot_general x12 -> x0, matrix products: 21 us -> none  [the longest x6 11.2 us: one_head(): jnp.einsum('fqd,fkd->fqk', query_head, picked_keys, preferred_element_typ...]
    dynamic_slice x12 -> x0, local copies, waits for them, and re-layouts: 13.2 us -> none  [the longest x6 9.42 us: one_head(): value_head = lax.dynamic_slice_in_dim(value_tiles, column_start, HDIM, 2)]
    another operation x3 -> x0, other arithmetic: 10.6 us -> none  [the longest x2 10.4 us: on_device(): window = jnp.stack([column_parts[0], row_strip, column_parts[1]])]
    slice x2 -> x0, local copies, waits for them, and re-layouts: 8.98 us -> none  [the longest x1 8.9 us: on_device(): value_tiles = window[:, :, 1].reshape(9 * frames, tile_len, feature_width)]
    gather x12 -> x0, local copies, waits for them, and re-layouts: 8.61 us -> none  [the longest x6 4.3 us: one_head(): jnp.take(value_head, source, axis=0)]
  transfers between devices with their start and end apart: 5 -> 0, of which waited for: 4 -> 0; matrix products, arithmetic and copies ran while one was open for 6% -> 0% of each run, Pallas kernels for 0% -> 0%
where the time goes in v1:
time: 64.6 us; the launch traced here: 64.4 us
  Pallas kernels  59.7 us (92%)
  local copies, waits for them, and re-layouts  4.66 us (7%)
    pallas_call x1, Pallas kernels, one_kernel(): pl.pallas_call(functools.partial(window_kernel, (tiles, chips), heads), o...  59.7 us
    unnamed x9, local copies, waits for them, and re-layouts  4.66 us

profile of v1, /device:TPU:0, one launch (start us, length us, event | category | flops | bytes accessed | tf_op | source)
XLA Modules:
  0.0 64.4 jit_solution(8755410508703703527)
XLA Ops:
  0.0 0.0 copy-start
  0.0 1.1 %copy-done = bf16[96,3072]{1,0:T(8,128)(2,1)S(1)} copy-done((bf16[96,3072]{1,0:T(8,128)(2,1)S(1)}, bf16[96,3072]{1,0:T(8,128)(2,1)}, u32[]{:S(2)}) %copy-start) | copy-done | bytes 589848
  1.1 0.0 copy-start.1
  1.1 1.1 %copy-done.1 = bf16[96,3072]{1,0:T(8,128)(2,1)S(1)} copy-done((bf16[96,3072]{1,0:T(8,128)(2,1)S(1)}, bf16[96,3072]{1,0:T(8,128)(2,1)}, u32[]{:S(2)}) %copy-start.1) | copy-done | bytes 589848
  2.1 0.0 copy-start.2
  2.1 1.1 %copy-done.2 = bf16[96,3072]{1,0:T(8,128)(2,1)S(1)} copy-done((bf16[96,3072]{1,0:T(8,128)(2,1)S(1)}, bf16[96,3072]{1,0:T(8,128)(2,1)}, u32[]{:S(2)}) %copy-start.2) | copy-done | bytes 589848
  3.2 0.0 copy-start.3
  3.2 0.7 %copy-done.3 = s32[1,27]{1,0:T(1,128)S(1)} copy-done((s32[1,27]{1,0:T(1,128)S(1)}, s32[1,27]{1,0:T(1,128)}, u32[]{:S(2)}) %copy-start.3) | copy-done | bytes 132
  3.9 59.7 %shard_map.46 = bf16[96,3072]{1,0:T(8,128)(2,1)S(1)} custom-call(bf16[96,3072]{1,0:T(8,128)(2,1)S(1)} %copy-done, bf16[96,3072]{1,0:T(8,128)(2,1)S(1)} %copy-done.1, bf16[96,3072]{1,0:T(8,128)(2,1)S(1)} %copy-done.2, s32[1,27]{1,0:T(1,128)S(1)} %copy-done.3), custom_call_target="tpu_custom_call" | custom-call | flops 1811939328 | bytes 2359296 | tf_op jit(solution)/shard_map/pallas_call | solution.py:319
  63.5 0.8 %copy.6 = bf16[96,3072]{1,0:T(8,128)(2,1)} copy(bf16[96,3072]{1,0:T(8,128)(2,1)S(1)} %shard_map.46) | data formatting | bytes 1179648
Async XLA Ops:
  0.0 1.1 %copy-start = (bf16[96,3072]{1,0:T(8,128)(2,1)S(1)}, bf16[96,3072]{1,0:T(8,128)(2,1)}, u32[]{:S(2)}) copy-start(bf16[96,3072]{1,0:T(8,128)(2,1)} %q_ref.1) | copy-start | bytes 1769476
  1.1 1.1 %copy-start.1 = (bf16[96,3072]{1,0:T(8,128)(2,1)S(1)}, bf16[96,3072]{1,0:T(8,128)(2,1)}, u32[]{:S(2)}) copy-start(bf16[96,3072]{1,0:T(8,128)(2,1)} %k_ref.1) | copy-start | bytes 1769476
  2.1 1.1 %copy-start.2 = (bf16[96,3072]{1,0:T(8,128)(2,1)S(1)}, bf16[96,3072]{1,0:T(8,128)(2,1)}, u32[]{:S(2)}) copy-start(bf16[96,3072]{1,0:T(8,128)(2,1)} %v_ref.1) | copy-start | bytes 1769476
  3.2 0.7 %copy-start.3 = (s32[1,27]{1,0:T(1,128)S(1)}, s32[1,27]{1,0:T(1,128)}, u32[]{:S(2)}) copy-start(s32[1,27]{1,0:T(1,128)} %m_ref.1) | copy-start | bytes 328

commit v2 on v1

--- a/solution.py
+++ b/solution.py
@@ -85,10 +85,11 @@
 
 MESH = pl.DeviceIdType.MESH
 MASKED = -1e30
+held_from = 2
 
 
 def window_kernel(
-    places, heads, q_ref, k_ref, v_ref, m_ref, out_ref, qbuf, kvbuf, obuf, mbuf, bias,
+    places, heads, q_ref, k_ref, v_ref, m_ref, out_ref, qbuf, kvbuf, obuf, mbuf, mrow, bias,
     in_send, in_recv, own_sem, pair_send, pair_recv, o_send, o_recv, o_own, m_send, m_recv,
 ):
     tiles, chips = places
@@ -107,8 +108,10 @@
         return pz * chips + px, {"ctx": pz, "head": px * 2 + core}
 
     sibling = {"ctx": z, "head": x * 2 + 1 - core}
-    distances = [2, 1, 3, 0]
-    offsets = [(dz, dx) for dz in distances for dx in range(chips) if (dz, dx) != (0, 0)]
+    odd = lax.rem(z, 2)
+    distances = [2, 3 - 2 * odd, 1 + 2 * odd]
+    offsets = [(dz, dx) for dz in distances for dx in range(chips)]
+    offsets += [(0, dx) for dx in range(1, chips)]
 
     def columns(place, h):
         return pl.ds(pl.multiple_of((place * heads + h) * HDIM, HDIM), HDIM)
@@ -136,8 +139,11 @@
             device_id_type=MESH,
         )
 
-    def in_arrival(kind, h, offset):
-        place, device = peer(*offset)
+    def query_arrival(h, pz, px):
+        return in_arrival(2, h, None, (pz * chips + px, {"ctx": pz, "head": px * 2 + core}))
+
+    def in_arrival(kind, h, offset, sender=None):
+        place, device = sender or peer(*offset)
         return pltpu.make_async_remote_copy(
             src_ref=sources[kind].at[:, columns(place, h)],
             dst_ref=slot(kind, h, place),
@@ -202,8 +208,11 @@
         pl.semaphore_signal(barrier, inc=1, device_id=peer(*offset)[1], device_id_type=MESH)
     pl.semaphore_signal(barrier, inc=1, device_id=sibling, device_id_type=MESH)
 
+    own_mask = pltpu.make_async_copy(m_ref, mrow, o_own.at[0])
+    own_mask.start()
+    own_mask.wait()
     mbuf[z] = jnp.zeros(mbuf.shape[1:], mbuf.dtype)
-    mbuf[z, 0:1, 0 : m_ref.shape[1]] = m_ref[...]
+    mbuf[z, 0:1, 0 : mrow.shape[1]] = mrow[...]
     pl.semaphore_wait(barrier, len(offsets) + 1)
 
     def start_head(h, carry):
@@ -214,11 +223,11 @@
         return carry
 
     start_head(0, 0)
-    for dz in distances[:-1]:
+    for dz in distances:
         mask_copy(dz, True).start()
     lax.fori_loop(1, heads, start_head, 0)
 
-    for dz in distances[:-1]:
+    for dz in distances:
         mask_copy(dz, False).wait_recv()
     grid_cols = 2
     spot = lax.broadcasted_iota(jnp.int32, (1, blocks * rows), 1)
@@ -262,30 +271,53 @@
         )
         obuf[h, pl.ds(start, tile_rows), :] = (mixed / total).astype(jnp.bfloat16)
 
+    def tile_at(i):
+        by_order = distances[2] * (i == 2) + distances[1] * (i == 1) + 2 * (i == 0)
+        return lax.rem(z + by_order, tiles)
+
+    def send_tile(h, pz):
+        for px in range(chips):
+            mine = pz * chips + px == here
+
+            @pl.when(jnp.logical_not(mine))
+            def _():
+                out_copy(h, pz, px).start()
+
+            @pl.when(mine)
+            def _():
+                out_own(h).start()
+
     def run_head(h, carry):
         for kind in range(2):
             for offset in offsets:
                 in_arrival(kind, h, offset).wait_recv()
             own_copy(kind, h).wait()
         pair_copy(h, core).start()
-        for offset in offsets:
-            in_arrival(2, h, offset).wait_recv()
-        own_copy(2, h).wait()
         pair_copy(h, 1 - core).wait_recv()
 
+        @pl.when(h == heads - 1)
+        def _():
+            for i in range(held_from, tiles):
+                send_tile(heads - 2, tile_at(i))
+
         def run_tile(i, carry):
-            pz = lax.rem(z + 2 + i, tiles)
-            attend(h, pz)
+            pz = tile_at(i)
             for px in range(chips):
                 mine = pz * chips + px == here
 
                 @pl.when(jnp.logical_not(mine))
                 def _():
-                    out_copy(h, pz, px).start()
+                    query_arrival(h, pz, px).wait_recv()
 
                 @pl.when(mine)
                 def _():
-                    out_own(h).start()
+                    own_copy(2, h).wait()
+
+            attend(h, pz)
+
+            @pl.when(jnp.logical_or(h != heads - 2, i < held_from))
+            def _():
+                send_tile(h, pz)
 
             return carry
 
@@ -304,7 +336,7 @@
         out_own(h).wait()
         return carry
 
-    for dz in distances[:-1]:
+    for dz in distances:
         mask_copy(dz, True).wait_send()
     lax.fori_loop(0, heads, finish_head, 0)
 
@@ -319,14 +351,14 @@
     return pl.pallas_call(
         functools.partial(window_kernel, (tiles, chips), heads),
         out_shape=jax.ShapeDtypeStruct((rows, width), jnp.bfloat16),
-        in_specs=[pl.BlockSpec(memory_space=pl.ANY)] * 3
-        + [pl.BlockSpec(memory_space=pltpu.VMEM)],
+        in_specs=[pl.BlockSpec(memory_space=pltpu.HBM)] * 4,
         out_specs=pl.BlockSpec(memory_space=pltpu.VMEM),
         scratch_shapes=[
             pltpu.VMEM((heads, blocks * rows, HDIM), jnp.bfloat16),
             pltpu.VMEM((heads, 2, 2, blocks * rows, HDIM), jnp.bfloat16),
             pltpu.VMEM((heads, blocks * rows, HDIM), jnp.bfloat16),
             pltpu.VMEM((tiles, 8, 128), jnp.int32),
+            pltpu.VMEM(tile_mask.shape, jnp.int32),
             pltpu.VMEM((tiles, 1, blocks * rows), jnp.float32),
             pltpu.SemaphoreType.DMA((heads, 3, blocks)),
             pltpu.SemaphoreType.DMA((heads, 3, blocks)),
@@ -340,7 +372,7 @@
             pltpu.SemaphoreType.DMA((tiles,)),
         ],
         compiler_params=pltpu.CompilerParams(
-            collective_id=0, has_side_effects=True, vmem_limit_bytes=48 * 1024 * 1024
+            collective_id=0, has_side_effects=True, vmem_limit_bytes=54272 * 1024
         ),
         cost_estimate=pl.CostEstimate(
             flops=flops, bytes_accessed=8 * rows * width, transcendentals=0

time: 64.6 us -> 60.3 us (0.933)
  local copies, waits for them, and re-layouts: 4.66 us -> 1.47 us
  Pallas kernels: 59.7 us -> 58.7 us
    unnamed x9 -> x3, local copies, waits for them, and re-layouts: 4.66 us -> 1.47 us
    pallas_call x1, Pallas kernels: 59.7 us -> 58.7 us  [one_kernel(): pl.pallas_call(functools.partial(window_kernel, (tiles, chips), heads), o...]
where the time goes in v2:
time: 60.3 us; the launch traced here: 60.2 us
  Pallas kernels  58.7 us (97%)
  local copies, waits for them, and re-layouts  1.47 us (2%)
    pallas_call x1, Pallas kernels, one_kernel(): pl.pallas_call(functools.partial(window_kernel, (tiles, chips), heads), o...  58.7 us
    unnamed x3, local copies, waits for them, and re-layouts  1.47 us

profile of v2, /device:TPU:0, one launch (start us, length us, event | category | flops | bytes accessed | tf_op | source)
XLA Modules:
  0.0 60.2 jit_solution(589699582007577756)
XLA Ops:
  0.0 0.0 copy-start
  0.0 0.7 %copy-done = s32[1,27]{1,0:T(1,128)S(1)} copy-done((s32[1,27]{1,0:T(1,128)S(1)}, s32[1,27]{1,0:T(1,128)}, u32[]{:S(2)}) %copy-start) | copy-done | bytes 132
  0.7 58.7 %shard_map.46 = bf16[96,3072]{1,0:T(8,128)(2,1)S(1)} custom-call(bf16[96,3072]{1,0:T(8,128)(2,1)} %q_ref.1, bf16[96,3072]{1,0:T(8,128)(2,1)} %k_ref.1, bf16[96,3072]{1,0:T(8,128)(2,1)} %v_ref.1, s32[1,27]{1,0:T(1,128)S(1)} %copy-done), custom_call_target="tpu_custom_call" | custom-call | flops 1811939328 | bytes 2359296 | tf_op jit(solution)/shard_map/pallas_call | solution.py:351
  59.4 0.8 %copy.6 = bf16[96,3072]{1,0:T(8,128)(2,1)} copy(bf16[96,3072]{1,0:T(8,128)(2,1)S(1)} %shard_map.46) | data formatting | bytes 1179648
Async XLA Ops:
  0.0 0.7 %copy-start = (s32[1,27]{1,0:T(1,128)S(1)}, s32[1,27]{1,0:T(1,128)}, u32[]{:S(2)}) copy-start(s32[1,27]{1,0:T(1,128)} %m_ref.1) | copy-start | bytes 328
